TPU v7x, 32 devices: a whole 2x2x4 slice. The times are simulated.
32 devices in a mesh: slab: 8 (over z, x), freq: 4 (over y, core).
Axes of the slice: x: 2, y: 2, z: 4, core: 2. Of those that a mesh axis runs over, the one named last changes fastest.
Arguments:
- source: bfloat16 [4, 2, 3, 64, 64, 128], P('freq', None, None, 'slab'), may hold values from -6 to 6
- omega: float32 [4], P('freq'), may hold values from 0.2 to 5
- sigma_blocks: float32 [256], replicated, may hold values from 0.25 to 4
- block_ids: int32 [64, 64, 128], P('slab'), may hold values from 0 to 255
- rec_owner: int32 [1024, 1], P('slab'), may hold values from 0 to 7; in each aligned block of 128 rows (0 to 127, 128 to 255, ...) at most 32 rows name the same one
- rec_edge: int32 [1024], P('slab'), may hold values from 0 to 196607
- observed: float32 [4, 2, 1024], P('freq', None, 'slab'), may hold values from -4 to 4
Outputs:
- forward_field: float32 [4, 2, 3, 64, 64, 128], P('freq', None, None, 'slab')
- adjoint_field: float32 [4, 2, 3, 64, 64, 128], P('freq', None, None, 'slab')
- gradient: float32 [256], replicated
Inputs may be any that keep to these rules, and one draw needn't show every extreme that they name: `rec_owner`: among the receiver rows of one slab device no slab is named more than 32 times; in some device's rows one slab is named exactly 32 times.
All inputs are finite; a program needn't handle non-finite values.
Results may differ from a plain program's by a relative error of at most 0.0003.
Values sent between devices are 32-bit elements; how exact they have to be, the bound alone decides.
A program may use at most 256 MiB of HBM per device.

v0:
```python
import jax
import jax.numpy as jnp
from jax import lax
from jax.sharding import PartitionSpec as P

SWEEPS = 4
epsilon = 1e-06


def extended(cells, sides, width):
    for axis, dim in sides:
        count = lax.axis_size(axis)
        ends = count - 1
        head = lax.slice_in_dim(cells, 0, width, axis=dim)
        tail = lax.slice_in_dim(cells, cells.shape[dim] - width, cells.shape[dim], axis=dim)
        cells = jnp.concatenate(
            [
                lax.ppermute(tail, axis, [(i, (i + 1) % count) for i in range(ends)]),
                cells,
                lax.ppermute(head, axis, [((i + 1) % count, i) for i in range(ends)]),
            ],
            axis=dim,
        )
    return cells


def forward_diff(values, along):
    along = along % values.ndim
    count = values.shape[along]
    ahead_values = jnp.concatenate(
        [
            lax.slice_in_dim(values, 1, count, axis=along),
            jnp.zeros_like(lax.slice_in_dim(values, 0, 1, axis=along)),
        ],
        axis=along,
    )
    return ahead_values - values


def adjoint_diff(values, along):
    along = along % values.ndim
    count = values.shape[along]
    behind = jnp.concatenate(
        [
            jnp.zeros_like(lax.slice_in_dim(values, 0, 1, axis=along)),
            lax.slice_in_dim(values, 0, count - 1, axis=along),
        ],
        axis=along,
    )
    return behind - values


def stiffness_of(field):
    padded = extended(field, (("slab", 3),), 1)
    edge_first = padded[:, :, 0]
    edge_second = padded[:, :, 1]
    edge_third = padded[:, :, 2]
    curl_first = forward_diff(edge_third[:, :, 1:-1], -2) - forward_diff(
        edge_second[:, :, 1:-1], -1
    )
    full_second = forward_diff(edge_first[:, :, :-1], -1) - (
        edge_third[:, :, 1:] - edge_third[:, :, :-1]
    )
    full_third = (
        edge_second[:, :, 1:] - edge_second[:, :, :-1] - forward_diff(edge_first[:, :, :-1], -2)
    )
    lower_valid = (lax.axis_index("slab") > 0).astype(jnp.float32)
    curl_second = jnp.concatenate(
        [full_second[:, :, :1] * lower_valid, full_second[:, :, 1:]], axis=2
    )
    curl_third = jnp.concatenate([full_third[:, :, :1] * lower_valid, full_third[:, :, 1:]], axis=2)
    back_first = adjoint_diff(curl_second[:, :, 1:], -1) - adjoint_diff(curl_third[:, :, 1:], -2)
    back_second = curl_third[:, :, :-1] - curl_third[:, :, 1:] - adjoint_diff(curl_first, -1)
    back_third = adjoint_diff(curl_first, -2) - (curl_second[:, :, :-1] - curl_second[:, :, 1:])
    return jnp.stack([back_first, back_second, back_third], axis=2)


def residual_sweeps(right_side, damping):
    denominator = 16.0 + damping * damping
    residual = right_side
    solution = jnp.zeros_like(right_side)
    for iteration in range(SWEEPS):
        residual_real = residual[:, 0]
        residual_imag = residual[:, 1]
        precond_real = (4.0 * residual_real + damping * residual_imag) / denominator
        precond_imag = (4.0 * residual_imag - damping * residual_real) / denominator
        stiffness = stiffness_of(jnp.stack([precond_real, precond_imag], axis=1))
        image_real = stiffness[:, 0] - damping * precond_imag
        image_imag = stiffness[:, 1] + damping * precond_real
        totals = lax.psum(
            (
                jnp.sum(image_real * residual_real + image_imag * residual_imag, axis=(1, 2, 3, 4)),
                jnp.sum(image_real * residual_imag - image_imag * residual_real, axis=(1, 2, 3, 4)),
                jnp.sum(image_real * image_real + image_imag * image_imag, axis=(1, 2, 3, 4)),
            ),
            "slab",
        )
        lower_sum = totals[2] + epsilon
        step_real = (totals[0] / lower_sum)[:, None, None, None, None]
        step_imag = (totals[1] / lower_sum)[:, None, None, None, None]
        solution = solution + jnp.stack(
            [
                step_real * precond_real - step_imag * precond_imag,
                step_real * precond_imag + step_imag * precond_real,
            ],
            axis=1,
        )
        residual = residual - jnp.stack(
            [
                step_real * image_real - step_imag * image_imag,
                step_real * image_imag + step_imag * image_real,
            ],
            axis=1,
        )
    return solution


def body(source, omega, sigma_blocks, block_ids, rec_owner, rec_edge, observed):
    conductivity = jnp.take(sigma_blocks, block_ids, axis=0)
    damping = omega[:, None, None, None, None] * conductivity[None, None]
    forward_field = residual_sweeps(source.astype(jnp.float32), damping)
    pair_count = forward_field.shape[0]
    flat_field = forward_field.reshape(pair_count, 2, -1)
    slab_count = lax.axis_size("slab")
    owner_slab = rec_owner[:, 0]
    local_count = rec_edge.shape[0]
    owner_hits = (owner_slab[:, None] == jnp.arange(slab_count, dtype=jnp.int32)[None, :]).astype(
        jnp.int32
    )
    earlier = jnp.cumsum(owner_hits, axis=0) - owner_hits
    slot_index = jnp.sum(earlier * owner_hits, axis=1)
    capacity = local_count // 4
    target = owner_slab * capacity + slot_index
    request = (
        jnp.full((slab_count * capacity,), -1, jnp.int32)
        .at[target]
        .set(rec_edge)
        .reshape(slab_count, capacity)
    )
    arrived = lax.all_to_all(request, "slab", split_axis=0, concat_axis=0, tiled=True)
    wanted = arrived.reshape(-1)
    present = (wanted >= 0).astype(jnp.float32)
    safe_edge = jnp.maximum(wanted, 0)
    picked = (jnp.take(flat_field, safe_edge, axis=2) * present).reshape(
        pair_count, 2, slab_count, capacity
    )
    returned = lax.all_to_all(picked, "slab", split_axis=2, concat_axis=2, tiled=True)
    predicted = jnp.take(returned.reshape(pair_count, 2, -1), target, axis=2)
    misfit = predicted - observed
    adjoint_data = jnp.stack([misfit[:, 0], -misfit[:, 1]], axis=1)
    outgoing = (
        jnp.zeros((pair_count, 2, slab_count * capacity), jnp.float32)
        .at[:, :, target]
        .set(adjoint_data)
        .reshape(pair_count, 2, slab_count, capacity)
    )
    incoming = lax.all_to_all(outgoing, "slab", split_axis=2, concat_axis=2, tiled=True)
    adjoint_flat = (
        jnp.zeros_like(flat_field)
        .at[:, :, safe_edge]
        .add(incoming.reshape(pair_count, 2, -1) * present)
    )
    adjoint_field = residual_sweeps(adjoint_flat.reshape(forward_field.shape), damping)
    cell_term = jnp.sum(
        omega[:, None, None, None]
        * jnp.sum(
            adjoint_field[:, 0] * forward_field[:, 1] + adjoint_field[:, 1] * forward_field[:, 0],
            axis=1,
        ),
        axis=0,
    )
    local_terms = jax.ops.segment_sum(
        cell_term.reshape(-1), block_ids.reshape(-1), num_segments=sigma_blocks.shape[0]
    )
    gradient = lax.psum(local_terms, ("slab", "freq"))
    return (forward_field, adjoint_field, gradient)


def solution(mesh):
    return jax.shard_map(
        body,
        mesh=mesh,
        in_specs=(
            P("freq", None, None, "slab", None, None),
            P("freq"),
            P(),
            P("slab", None, None),
            P("slab", None),
            P("slab"),
            P("freq", None, "slab"),
        ),
        out_specs=(
            P("freq", None, None, "slab", None, None),
            P("freq", None, None, "slab", None, None),
            P(),
        ),
        check_vma=False,
    )
```

profile of v0, /device:TPU:14, one launch (start us, length us, event | category | flops | bytes accessed | tf_op | source)
XLA Modules:
  0.0 1428.3 jit_solution(17710169639621398789)
XLA Ops:
  2.8 406.1 %gather_fusion = f32[65536]{0:T(1024)S(1)} fusion(f32[256]{0:T(256)S(1)} %copy-done, s32[65536]{0:T(1024)S(1)} %broadcast_clamp_fusion), kind=kCustom, calls=%fused_computation | custom fusion | bytes 786432 | tf_op jit(solution)/shard_map/jit(_take)/gather | solution.py:119
  430.8 14.9 %all-reduce.71 = (f32[1]{0:T(128)}, f32[1]{0:T(128)}, f32[1]{0:T(128)}) all-reduce(f32[1]{0:T(128)} %bitcast.16, f32[1]{0:T(128)} %bitcast.14, f32[1]{0:T(128)} %bitcast.13), channel_id=1, replica_groups=mesh['slab'=8,'freq'=4] {'slab'}, use_global_device_ids=true, to_apply=%region_5.6 | all-reduce | flops 3 | bytes 24 | tf_op jit(solution)/shard_map/psum | solution.py:90
  453.6 4.3 collective-permute-start.3
  462.2 8.1 all-to-all-start
  476.7 15.7 %all-reduce.70 = (f32[1]{0:T(128)}, f32[1]{0:T(128)}, f32[1]{0:T(128)}) all-reduce(f32[1]{0:T(128)} %bitcast.32, f32[1]{0:T(128)} %bitcast.30, f32[1]{0:T(128)} %bitcast.29), channel_id=1, replica_groups=mesh['slab'=8,'freq'=4] {'slab'}, use_global_device_ids=true, to_apply=%region_11.12 | all-reduce | flops 3 | bytes 24 | tf_op jit(solution)/shard_map/psum | solution.py:90
  500.5 6.1 collective-permute-start.5
  509.8 4.5 collective-permute-done.4
  520.6 17.6 %all-reduce.69 = (f32[1]{0:T(128)}, f32[1]{0:T(128)}, f32[1]{0:T(128)}) all-reduce(f32[1]{0:T(128)} %bitcast.48, f32[1]{0:T(128)} %bitcast.46, f32[1]{0:T(128)} %bitcast.45), channel_id=1, replica_groups=mesh['slab'=8,'freq'=4] {'slab'}, use_global_device_ids=true, to_apply=%region_17.18 | all-reduce | flops 3 | bytes 24 | tf_op jit(solution)/shard_map/psum | solution.py:90
  561.4 17.1 %all-reduce.68 = (f32[1]{0:T(128)}, f32[1]{0:T(128)}, f32[1]{0:T(128)}) all-reduce(f32[1]{0:T(128)} %bitcast.64, f32[1]{0:T(128)} %bitcast.62, f32[1]{0:T(128)} %bitcast.61), channel_id=1, replica_groups=mesh['slab'=8,'freq'=4] {'slab'}, use_global_device_ids=true, to_apply=%region_23.24 | all-reduce | flops 3 | bytes 24 | tf_op jit(solution)/shard_map/psum | solution.py:90
  582.8 5.9 fusion.7
  588.7 44.4 %copy.224 = f32[2,196608]{0,1:T(8,128)} copy(f32[2,196608]{1,0:T(2,128)S(1)} %fusion.7) | data formatting | bytes 3145728 | tf_op jit(solution)/shard_map/add | solution.py:101
  633.1 4.9 gather_fusion.1
  638.8 10.6 all-to-all-start.1
  656.1 5.6 all-to-all-start.2
  666.2 44.5 %scatter_custom_fusion.2 = f32[2,196608]{0,1:T(8,128)} fusion(s32[256]{0:T(256)S(1)} %get-tuple-element.3, f32[]{:T(128)} %constant.38.clone.1, f32[256,2]{1,0:T(8,128)S(1)} %copy.232, s32[1024]{0:T(1024)S(1)} %pad_clamp_fusion), kind=kCustom, calls=%fused_computation.8 | custom fusion | flops 512 | bytes 1572868 | tf_op jit(solution)/shard_map/scatter-add | solution.py:161
  710.7 57.2 %copy.233 = f32[1,2,3,8,64,128]{5,4,3,2,1,0:T(8,128)S(1)} copy(f32[1,2,3,8,64,128]{1,5,4,3,2,0:T(8,128)} %bitcast.92) | data formatting | bytes 3145728 | tf_op jit(solution)/shard_map/reshape | solution.py:163
  783.8 17.1 %all-reduce.67 = (f32[1]{0:T(128)}, f32[1]{0:T(128)}, f32[1]{0:T(128)}) all-reduce(f32[1]{0:T(128)} %bitcast.106, f32[1]{0:T(128)} %bitcast.104, f32[1]{0:T(128)} %bitcast.103), channel_id=1, replica_groups=mesh['slab'=8,'freq'=4] {'slab'}, use_global_device_ids=true, to_apply=%region_34.35 | all-reduce | flops 3 | bytes 24 | tf_op jit(solution)/shard_map/psum | solution.py:90
  823.8 17.1 %all-reduce.66 = (f32[1]{0:T(128)}, f32[1]{0:T(128)}, f32[1]{0:T(128)}) all-reduce(f32[1]{0:T(128)} %bitcast.122, f32[1]{0:T(128)} %bitcast.120, f32[1]{0:T(128)} %bitcast.119), channel_id=1, replica_groups=mesh['slab'=8,'freq'=4] {'slab'}, use_global_device_ids=true, to_apply=%region_40.41 | all-reduce | flops 3 | bytes 24 | tf_op jit(solution)/shard_map/psum | solution.py:90
  856.0 5.7 collective-permute-done.12
  866.3 17.7 %all-reduce.65 = (f32[1]{0:T(128)}, f32[1]{0:T(128)}, f32[1]{0:T(128)}) all-reduce(f32[1]{0:T(128)} %bitcast.138, f32[1]{0:T(128)} %bitcast.136, f32[1]{0:T(128)} %bitcast.135), channel_id=1, replica_groups=mesh['slab'=8,'freq'=4] {'slab'}, use_global_device_ids=true, to_apply=%region_46.47 | all-reduce | flops 3 | bytes 24 | tf_op jit(solution)/shard_map/psum | solution.py:90
  890.6 4.7 collective-permute-start.15
  907.2 17.2 %all-reduce.64 = (f32[1]{0:T(128)}, f32[1]{0:T(128)}, f32[1]{0:T(128)}) all-reduce(f32[1]{0:T(128)} %bitcast.154, f32[1]{0:T(128)} %bitcast.152, f32[1]{0:T(128)} %bitcast.151), channel_id=1, replica_groups=mesh['slab'=8,'freq'=4] {'slab'}, use_global_device_ids=true, to_apply=%region_52.53 | all-reduce | flops 3 | bytes 24 | tf_op jit(solution)/shard_map/psum | solution.py:90
  931.3 452.6 %scatter_custom_fusion.3 = f32[256]{0:T(256)S(1)} fusion(s32[65536]{0:T(1024)} %bitcast.724, f32[65536]{0:T(1024)S(1)} %bitcast.727, f32[]{:T(128)} %constant.38.clone.1), kind=kCustom, calls=%fused_computation.483 | custom fusion | flops 65536 | bytes 1536 | tf_op jit(solution)/shard_map/scatter-add | solution.py:172
  1383.9 43.9 %psum.199 = f32[256]{0:T(256)} all-reduce(f32[256]{0:T(256)S(1)} %scatter_custom_fusion.3), channel_id=1, replica_groups=mesh['slab'=8,'freq'=4] {'slab','freq'}, use_global_device_ids=true, to_apply=%region_55.56 | all-reduce | flops 256 | bytes 2048 | tf_op jit(solution)/shard_map/psum | solution.py:175
  (358 shorter events, 166.4 us)
Async XLA Ops:
  409.2 16.8 %copy-start.9 = (f32[1,1,3,8,64,128]{5,4,3,2,1,0:T(8,128)}, f32[1,1,3,8,64,128]{5,4,3,2,1,0:T(8,128)S(1)}, u32[]{:S(2)}) copy-start(f32[1,1,3,8,64,128]{5,4,3,2,1,0:T(8,128)S(1)} %get-tuple-element.99) | copy-start | bytes 2359300
  410.8 11.1 collective-permute-start.1
  413.2 11.5 collective-permute-start
  453.6 16.7 %collective-permute-start.3 = (f32[1,2,3,1,64,128]{5,4,3,2,1,0:T(8,128)S(1)}, f32[1,2,3,1,64,128]{5,4,3,2,1,0:T(8,128)S(1)}, u32[]{:S(2)}, u32[]{:S(2)}) collective-permute-start(f32[1,2,3,1,64,128]{5,4,3,2,1,0:T(8,128)S(1)} %get-tuple-element.152), channel_id=1, source_target_pairs={{4,0},{8,4},{12,8},{16,12},{20,16},{24,20},{28,24},{5,1},{9,5},{13... | collective-permute-start | bytes 589832 | tf_op jit(solution)/shard_map/ppermute | solution.py:20
  458.0 12.4 collective-permute-start.2
  462.2 46.6 %all-to-all-start = ((s32[8,1,32]{2,1,0:T(1,128)}), s32[8,1,32]{2,1,0:T(1,128)S(1)}, u32[]{:S(2)}, u32[]{:S(2)}) async-start(s32[8,1,32]{2,1,0:T(1,128)} %all_to_all.12), calls=%async_computation | async-start | bytes 8192 | tf_op jit(solution)/shard_map/all_to_all | solution.py:140
  500.5 9.2 collective-permute-start.5
  506.6 7.7 collective-permute-start.4
  544.8 8.5 collective-permute-start.7
  549.0 8.1 collective-permute-start.6
  560.0 21.8 %copy-start.50 = (f32[1,1,3,8,64,128]{5,4,3,2,1,0:T(8,128)S(1)}, f32[1,1,3,8,64,128]{5,4,3,2,1,0:T(8,128)}, u32[]{:S(2)}) copy-start(f32[1,1,3,8,64,128]{5,4,3,2,1,0:T(8,128)} %get-tuple-element.145) | copy-start | bytes 2359300
  588.7 65.7 %copy-start.62 = (f32[1,2,128]{2,1,0:T(2,128)S(1)}, f32[1,2,128]{2,1,0:T(2,128)}, u32[]{:S(2)}) copy-start(f32[1,2,128]{2,1,0:T(2,128)} %param.13) | copy-start | bytes 3076
  638.8 14.8 %all-to-all-start.1 = ((f32[1,2,8,32]{3,1,0,2:T(2,128)}), f32[1,2,8,32]{3,1,0,2:T(2,128)S(1)}, u32[]{:S(2)}, u32[]{:S(2)}) async-start(f32[1,2,8,32]{3,1,0,2:T(2,128)} %select_multiply_fusion.1), calls=%async_computation.1 | async-start | bytes 16384 | tf_op jit(solution)/shard_map/all_to_all | solution.py:147
  656.1 9.8 all-to-all-start.2
  768.2 8.5 collective-permute-start.9
  771.3 7.6 collective-permute-start.8
  807.5 8.5 collective-permute-start.11
  810.8 8.1 collective-permute-start.10
  847.5 8.5 collective-permute-start.13
  851.6 10.0 collective-permute-start.12
  890.6 9.2 collective-permute-start.15
  895.2 7.8 collective-permute-start.14
  905.9 20.6 %copy-start.59 = (f32[1,1,3,8,64,128]{5,4,3,2,1,0:T(8,128)S(1)}, f32[1,1,3,8,64,128]{5,4,3,2,1,0:T(8,128)}, u32[]{:S(2)}) copy-start(f32[1,1,3,8,64,128]{5,4,3,2,1,0:T(8,128)} %get-tuple-element.129) | copy-start | bytes 2359300
  928.1 499.7 %copy-start.1 = (f32[256]{0:T(256)S(1)}, f32[256]{0:T(256)}, u32[]{:S(2)}) copy-start(f32[256]{0:T(256)} %param.9) | copy-start | bytes 3076
  (58 other events, 195.9 us)
where the time goes:
time: 1440 us; the launch traced here: 1430 us
  other arithmetic  570 us (40%)
  local copies, waits for them, and re-layouts  539 us (37%)
  blocking collectives  178 us (12%)
  starting transfers between devices  80.4 us (6%)
  waiting for transfers between devices  42.3 us (3%)
  between operations  18.4 us (1%)
    scatter-add x1, other arithmetic, body(): jax.ops.segment_sum(cell_term.reshape(-1), block_ids.reshape(-1), num_seg...  453 us
    gather x1, local copies, waits for them, and re-layouts, body(): conductivity = jnp.take(sigma_blocks, block_ids, axis=0)  406 us
    psum x8, blocking collectives, residual_sweeps(): lax.psum((jnp.sum(image_real * residual_real + image_imag * residual_imag...  134 us
    reshape x1, local copies, waits for them, and re-layouts, body(): adjoint_flat.reshape(forward_field.shape)  57.2 us
    scatter-add x3, other arithmetic, body(): adjoint_flat = jnp.zeros_like(flat_field).at[:, :, safe_edge].add(incomin...  47.1 us
    add x1, local copies, waits for them, and re-layouts, residual_sweeps(): solution + jnp.stack([step_real * precond_real - step_imag * precond_imag...  44.4 us
    psum x1, blocking collectives, body(): gradient = lax.psum(local_terms, ('slab', 'freq'))  43.9 us
    ppermute x8, starting transfers between devices, extended(): lax.ppermute(head, axis, [((i + 1) % count, i) for i in range(ends)])  32.2 us
  transfers between devices with their start and end apart: 19, of which 15 were waited for; matrix products, arithmetic and copies ran while one was open for 1% of the time, Pallas kernels for 0%

commit v1 on v0

--- a/solution.py
+++ b/solution.py
@@ -172,7 +172,7 @@
     local_terms = jax.ops.segment_sum(
         cell_term.reshape(-1), block_ids.reshape(-1), num_segments=sigma_blocks.shape[0]
     )
-    gradient = lax.psum(local_terms, ("slab", "freq"))
+    gradient = lax.psum(lax.psum(local_terms, "freq"), "slab")
     return (forward_field, adjoint_field, gradient)
 
 

time: 1440 us -> 1420 us (0.986)
  blocking collectives: 178 us -> 160 us
    psum x1 -> x2, blocking collectives: 43.9 us -> 26 us  [body(): gradient = lax.psum(lax.psum(local_terms, 'freq'), 'slab')]
where the time goes in v1:
time: 1420 us; the launch traced here: 1410 us
  other arithmetic  570 us (40%)
  local copies, waits for them, and re-layouts  539 us (38%)
  blocking collectives  160 us (11%)
  starting transfers between devices  80.6 us (6%)
  waiting for transfers between devices  42.4 us (3%)
  between operations  18.5 us (1%)
    scatter-add x1, other arithmetic, body(): jax.ops.segment_sum(cell_term.reshape(-1), block_ids.reshape(-1), num_seg...  453 us
    gather x1, local copies, waits for them, and re-layouts, body(): conductivity = jnp.take(sigma_blocks, block_ids, axis=0)  406 us
    psum x8, blocking collectives, residual_sweeps(): lax.psum((jnp.sum(image_real * residual_real + image_imag * residual_imag...  134 us
    reshape x1, local copies, waits for them, and re-layouts, body(): adjoint_flat.reshape(forward_field.shape)  57.2 us
    scatter-add x3, other arithmetic, body(): adjoint_flat = jnp.zeros_like(flat_field).at[:, :, safe_edge].add(incomin...  47.1 us
    add x1, local copies, waits for them, and re-layouts, residual_sweeps(): solution + jnp.stack([step_real * precond_real - step_imag * precond_imag...  44.5 us
    ppermute x8, starting transfers between devices, extended(): lax.ppermute(head, axis, [((i + 1) % count, i) for i in range(ends)])  32.5 us
  transfers between devices with their start and end apart: 19, of which 15 were waited for; matrix products, arithmetic and copies ran while one was open for 1% of the time, Pallas kernels for 0%

profile of v1, /device:TPU:14, one launch (start us, length us, event | category | flops | bytes accessed | tf_op | source)
XLA Modules:
  0.0 1410.3 jit_solution(14579306841632204684)
XLA Ops:
  2.8 406.1 %gather_fusion = f32[65536]{0:T(1024)S(1)} fusion(f32[256]{0:T(256)S(1)} %copy-done, s32[65536]{0:T(1024)S(1)} %broadcast_clamp_fusion), kind=kCustom, calls=%fused_computation | custom fusion | bytes 786432 | tf_op jit(solution)/shard_map/jit(_take)/gather | solution.py:119
  430.7 14.9 %all-reduce.71 = (f32[1]{0:T(128)}, f32[1]{0:T(128)}, f32[1]{0:T(128)}) all-reduce(f32[1]{0:T(128)} %bitcast.16, f32[1]{0:T(128)} %bitcast.14, f32[1]{0:T(128)} %bitcast.13), channel_id=1, replica_groups=mesh['slab'=8,'freq'=4] {'slab'}, use_global_device_ids=true, to_apply=%region_5.6 | all-reduce | flops 3 | bytes 24 | tf_op jit(solution)/shard_map/psum | solution.py:90
  462.3 8.1 all-to-all-start
  476.7 15.7 %all-reduce.70 = (f32[1]{0:T(128)}, f32[1]{0:T(128)}, f32[1]{0:T(128)}) all-reduce(f32[1]{0:T(128)} %bitcast.32, f32[1]{0:T(128)} %bitcast.30, f32[1]{0:T(128)} %bitcast.29), channel_id=1, replica_groups=mesh['slab'=8,'freq'=4] {'slab'}, use_global_device_ids=true, to_apply=%region_11.12 | all-reduce | flops 3 | bytes 24 | tf_op jit(solution)/shard_map/psum | solution.py:90
  500.4 6.1 collective-permute-start.5
  520.5 17.2 %all-reduce.69 = (f32[1]{0:T(128)}, f32[1]{0:T(128)}, f32[1]{0:T(128)}) all-reduce(f32[1]{0:T(128)} %bitcast.48, f32[1]{0:T(128)} %bitcast.46, f32[1]{0:T(128)} %bitcast.45), channel_id=1, replica_groups=mesh['slab'=8,'freq'=4] {'slab'}, use_global_device_ids=true, to_apply=%region_17.18 | all-reduce | flops 3 | bytes 24 | tf_op jit(solution)/shard_map/psum | solution.py:90
  544.4 4.6 collective-permute-start.7
  560.9 17.3 %all-reduce.68 = (f32[1]{0:T(128)}, f32[1]{0:T(128)}, f32[1]{0:T(128)}) all-reduce(f32[1]{0:T(128)} %bitcast.64, f32[1]{0:T(128)} %bitcast.62, f32[1]{0:T(128)} %bitcast.61), channel_id=1, replica_groups=mesh['slab'=8,'freq'=4] {'slab'}, use_global_device_ids=true, to_apply=%region_23.24 | all-reduce | flops 3 | bytes 24 | tf_op jit(solution)/shard_map/psum | solution.py:90
  582.5 5.9 fusion.7
  588.4 44.5 %copy.224 = f32[2,196608]{0,1:T(8,128)} copy(f32[2,196608]{1,0:T(2,128)S(1)} %fusion.7) | data formatting | bytes 3145728 | tf_op jit(solution)/shard_map/add | solution.py:101
  632.9 4.9 gather_fusion.1
  638.5 10.9 all-to-all-start.1
  656.2 5.6 all-to-all-start.2
  666.2 44.5 %scatter_custom_fusion.2 = f32[2,196608]{0,1:T(8,128)} fusion(s32[256]{0:T(256)S(1)} %get-tuple-element.3, f32[]{:T(128)} %constant.38.clone.1, f32[256,2]{1,0:T(8,128)S(1)} %copy.232, s32[1024]{0:T(1024)S(1)} %pad_clamp_fusion), kind=kCustom, calls=%fused_computation.8 | custom fusion | flops 512 | bytes 1572868 | tf_op jit(solution)/shard_map/scatter-add | solution.py:161
  710.8 57.2 %copy.233 = f32[1,2,3,8,64,128]{5,4,3,2,1,0:T(8,128)S(1)} copy(f32[1,2,3,8,64,128]{1,5,4,3,2,0:T(8,128)} %bitcast.92) | data formatting | bytes 3145728 | tf_op jit(solution)/shard_map/reshape | solution.py:163
  783.8 17.1 %all-reduce.67 = (f32[1]{0:T(128)}, f32[1]{0:T(128)}, f32[1]{0:T(128)}) all-reduce(f32[1]{0:T(128)} %bitcast.106, f32[1]{0:T(128)} %bitcast.104, f32[1]{0:T(128)} %bitcast.103), channel_id=1, replica_groups=mesh['slab'=8,'freq'=4] {'slab'}, use_global_device_ids=true, to_apply=%region_34.35 | all-reduce | flops 3 | bytes 24 | tf_op jit(solution)/shard_map/psum | solution.py:90
  823.7 17.1 %all-reduce.66 = (f32[1]{0:T(128)}, f32[1]{0:T(128)}, f32[1]{0:T(128)}) all-reduce(f32[1]{0:T(128)} %bitcast.122, f32[1]{0:T(128)} %bitcast.120, f32[1]{0:T(128)} %bitcast.119), channel_id=1, replica_groups=mesh['slab'=8,'freq'=4] {'slab'}, use_global_device_ids=true, to_apply=%region_40.41 | all-reduce | flops 3 | bytes 24 | tf_op jit(solution)/shard_map/psum | solution.py:90
  856.1 5.7 collective-permute-done.12
  866.5 17.7 %all-reduce.65 = (f32[1]{0:T(128)}, f32[1]{0:T(128)}, f32[1]{0:T(128)}) all-reduce(f32[1]{0:T(128)} %bitcast.138, f32[1]{0:T(128)} %bitcast.136, f32[1]{0:T(128)} %bitcast.135), channel_id=1, replica_groups=mesh['slab'=8,'freq'=4] {'slab'}, use_global_device_ids=true, to_apply=%region_46.47 | all-reduce | flops 3 | bytes 24 | tf_op jit(solution)/shard_map/psum | solution.py:90
  890.7 4.6 collective-permute-start.15
  907.3 17.1 %all-reduce.64 = (f32[1]{0:T(128)}, f32[1]{0:T(128)}, f32[1]{0:T(128)}) all-reduce(f32[1]{0:T(128)} %bitcast.154, f32[1]{0:T(128)} %bitcast.152, f32[1]{0:T(128)} %bitcast.151), channel_id=1, replica_groups=mesh['slab'=8,'freq'=4] {'slab'}, use_global_device_ids=true, to_apply=%region_52.53 | all-reduce | flops 3 | bytes 24 | tf_op jit(solution)/shard_map/psum | solution.py:90
  931.3 452.6 %scatter_custom_fusion.3 = f32[256]{0:T(256)S(1)} fusion(s32[65536]{0:T(1024)} %bitcast.724, f32[65536]{0:T(1024)S(1)} %bitcast.727, f32[]{:T(128)} %constant.38.clone.1), kind=kCustom, calls=%fused_computation.483 | custom fusion | flops 65536 | bytes 1536 | tf_op jit(solution)/shard_map/scatter-add | solution.py:172
  1383.9 5.9 psum.206
  1389.8 20.1 %psum.207 = f32[256]{0:T(256)} all-reduce(f32[256]{0:T(256)S(1)} %psum.206), channel_id=1, replica_groups=mesh['slab'=8,'freq'=4] {'slab'}, use_global_device_ids=true, to_apply=%region_56.57 | all-reduce | flops 256 | bytes 2048 | tf_op jit(solution)/shard_map/psum | solution.py:175
  (359 shorter events, 170.5 us)
Async XLA Ops:
  409.2 16.8 %copy-start.9 = (f32[1,1,3,8,64,128]{5,4,3,2,1,0:T(8,128)}, f32[1,1,3,8,64,128]{5,4,3,2,1,0:T(8,128)S(1)}, u32[]{:S(2)}) copy-start(f32[1,1,3,8,64,128]{5,4,3,2,1,0:T(8,128)S(1)} %get-tuple-element.99) | copy-start | bytes 2359300
  410.8 11.1 collective-permute-start.1
  413.2 11.5 collective-permute-start
  453.8 16.6 %collective-permute-start.3 = (f32[1,2,3,1,64,128]{5,4,3,2,1,0:T(8,128)S(1)}, f32[1,2,3,1,64,128]{5,4,3,2,1,0:T(8,128)S(1)}, u32[]{:S(2)}, u32[]{:S(2)}) collective-permute-start(f32[1,2,3,1,64,128]{5,4,3,2,1,0:T(8,128)S(1)} %get-tuple-element.152), channel_id=1, source_target_pairs={{4,0},{8,4},{12,8},{16,12},{20,16},{24,20},{28,24},{5,1},{9,5},{13... | collective-permute-start | bytes 589832 | tf_op jit(solution)/shard_map/ppermute | solution.py:20
  458.1 12.3 collective-permute-start.2
  462.3 46.4 %all-to-all-start = ((s32[8,1,32]{2,1,0:T(1,128)}), s32[8,1,32]{2,1,0:T(1,128)S(1)}, u32[]{:S(2)}, u32[]{:S(2)}) async-start(s32[8,1,32]{2,1,0:T(1,128)} %all_to_all.12), calls=%async_computation | async-start | bytes 8192 | tf_op jit(solution)/shard_map/all_to_all | solution.py:140
  500.4 9.2 collective-permute-start.5
  506.5 7.7 collective-permute-start.4
  544.4 8.5 collective-permute-start.7
  549.0 7.7 collective-permute-start.6
  559.6 21.9 %copy-start.50 = (f32[1,1,3,8,64,128]{5,4,3,2,1,0:T(8,128)S(1)}, f32[1,1,3,8,64,128]{5,4,3,2,1,0:T(8,128)}, u32[]{:S(2)}) copy-start(f32[1,1,3,8,64,128]{5,4,3,2,1,0:T(8,128)} %get-tuple-element.145) | copy-start | bytes 2359300
  588.4 66.0 %copy-start.62 = (f32[1,2,128]{2,1,0:T(2,128)S(1)}, f32[1,2,128]{2,1,0:T(2,128)}, u32[]{:S(2)}) copy-start(f32[1,2,128]{2,1,0:T(2,128)} %param.13) | copy-start | bytes 3076
  638.5 15.1 %all-to-all-start.1 = ((f32[1,2,8,32]{3,1,0,2:T(2,128)}), f32[1,2,8,32]{3,1,0,2:T(2,128)S(1)}, u32[]{:S(2)}, u32[]{:S(2)}) async-start(f32[1,2,8,32]{3,1,0,2:T(2,128)} %select_multiply_fusion.1), calls=%async_computation.1 | async-start | bytes 16384 | tf_op jit(solution)/shard_map/all_to_all | solution.py:147
  656.2 9.8 all-to-all-start.2
  768.2 8.5 collective-permute-start.9
  771.4 7.6 collective-permute-start.8
  807.5 8.5 collective-permute-start.11
  810.8 8.1 collective-permute-start.10
  847.6 8.5 collective-permute-start.13
  851.7 10.0 collective-permute-start.12
  890.7 9.2 collective-permute-start.15
  895.3 7.8 collective-permute-start.14
  906.1 20.5 %copy-start.59 = (f32[1,1,3,8,64,128]{5,4,3,2,1,0:T(8,128)S(1)}, f32[1,1,3,8,64,128]{5,4,3,2,1,0:T(8,128)}, u32[]{:S(2)}) copy-start(f32[1,1,3,8,64,128]{5,4,3,2,1,0:T(8,128)} %get-tuple-element.129) | copy-start | bytes 2359300
  928.1 481.7 %copy-start.1 = (f32[256]{0:T(256)S(1)}, f32[256]{0:T(256)}, u32[]{:S(2)}) copy-start(f32[256]{0:T(256)} %param.9) | copy-start | bytes 3076
  (58 other events, 196.1 us)
